TPU v7x, 32 devices: a whole 2x2x4 slice. The times are simulated.
32 devices in a mesh: cells: 8 (over z, y), genes: 4 (over x, core).
Axes of the slice: x: 2, y: 2, z: 4, core: 2. Of those that a mesh axis runs over, the one named last changes fastest.
Arguments:
- counts: bfloat16 [1024, 16384], P('cells', 'genes'), may hold values from 0 to 254
- occupancy: int32 [8, 128], P('cells', 'genes'), may hold values 0 or 1
- start_basis: bfloat16 [64, 16384], P(None, 'genes'), may hold values from -0.046875 to 0.046875
Outputs:
- new_basis: float32 [64, 16384], P(None, ('genes', 'cells'))
All inputs are finite; a program needn't handle non-finite values. No bound on the sum of `occupancy` on one device may be relied on, other than what follows from the above.
Results may differ from a plain program's by a relative error of at most 0.01.
Values sent between devices are 32-bit elements; how exact they have to be, the bound alone decides.
No kernel may reach another device: no remote copies, remote signals or barrier semaphores. Data moves between devices by JAX's collectives and lax.ppermute only.
A program may use at most 64 MiB of HBM per device.

v0:
```python
import functools
import math

import jax
import jax.numpy as jnp
from jax import lax
from jax.experimental import pallas as pl
from jax.experimental.pallas import tpu as pltpu
from jax.sharding import PartitionSpec as P

F32 = jnp.float32
BF16 = jnp.bfloat16
NN = (((1,), (0,)), ((), ()))
NT = (((1,), (1,)), ((), ()))
WHOLE = pl.BlockSpec(memory_space=pltpu.VMEM)
SCALARS = pl.BlockSpec(memory_space=pltpu.SMEM)
LANES = 128
PARAMS = pltpu.CompilerParams(vmem_limit_bytes=16 * 2**20)
LOG_PARAMS = pltpu.CompilerParams(vmem_limit_bytes=205 * 2**18)


def dot(a, b, dims):
    return lax.dot_general(a, b, dims, preferred_element_type=F32)


def split_terms(x, count):
    terms = []
    for _ in range(count):
        term = x.astype(BF16)
        terms.append(term)
        x = x - term.astype(F32)
    return terms


def tree_sum(parts):
    while len(parts) > 1:
        parts = [sum(parts[at + 1:at + 2], parts[at]) for at in range(0, len(parts), 2)]
    return parts[0]


def log_kernel(width, counts_hbm, high_ref, low_ref, sum_ref, counts_ref, counts_sem):
    cells, genes = high_ref.shape
    fetches = [
        pltpu.make_async_copy(
            counts_hbm.at[:, pl.ds(at * width, width)], counts_ref.at[:, pl.ds(at * width, width)], counts_sem.at[at]
        )
        for at in range(genes // width)
    ]
    for fetch in fetches:
        fetch.start()
    for at, fetch in enumerate(fetches):
        fetch.wait()
        for begin in range(at * width, (at + 1) * width, LANES):
            lanes = pl.ds(begin, LANES)
            logged = jnp.log(1.0 + counts_ref[:, lanes].astype(F32))
            high = logged.astype(BF16)
            high_ref[:, lanes] = high
            low_ref[:, lanes] = (logged - high.astype(F32)).astype(BF16)
            sum_ref[:, lanes] = jnp.sum(logged, axis=0, keepdims=True)


def log_terms(counts):
    cells, genes = counts.shape
    width = genes // 8
    return pl.pallas_call(
        functools.partial(log_kernel, width),
        out_shape=(
            jax.ShapeDtypeStruct((cells, genes), BF16),
            jax.ShapeDtypeStruct((cells, genes), BF16),
            jax.ShapeDtypeStruct((1, genes), F32),
        ),
        in_specs=[pl.BlockSpec(memory_space=pltpu.HBM)],
        out_specs=(WHOLE, WHOLE, WHOLE),
        scratch_shapes=[pltpu.VMEM(counts.shape, BF16), pltpu.SemaphoreType.DMA((genes // width,))],
        compiler_params=LOG_PARAMS,
        cost_estimate=pl.CostEstimate(flops=20 * cells * genes, bytes_accessed=8 * cells * genes, transcendentals=0),
        name="log_terms",
    )(counts)


def score_kernel(width, occ_ref, basis_ref, high_ref, low_ref, score_ref, lane_ref):
    comps, genes = basis_ref.shape
    edge = genes // occ_ref.shape[1]
    occupancy = occ_ref[...].astype(F32)
    scores = None
    for begin in range(0, genes, width):
        basis = []
        for at in range(begin, begin + width, edge):
            occ = jnp.broadcast_to(occupancy[:, at // edge:at // edge + 1], (1, edge))
            lane_ref[:, pl.ds(at, edge)] = occ
            basis.append(basis_ref[:, pl.ds(at, edge)] * occ.astype(BF16))
        basis = jnp.concatenate(basis, axis=1)
        lanes = pl.ds(begin, width)
        part = dot(basis, high_ref[:, lanes], NT) + dot(basis, low_ref[:, lanes], NT)
        scores = part if scores is None else scores + part
    score_ref[...] = scores


def score_part(occupancy, basis, high, low):
    comps, genes = basis.shape
    cells = high.shape[0]
    return pl.pallas_call(
        functools.partial(score_kernel, genes // 4),
        out_shape=(jax.ShapeDtypeStruct((comps, cells), F32), jax.ShapeDtypeStruct((1, genes), F32)),
        in_specs=[WHOLE] * 4,
        out_specs=(WHOLE, WHOLE),
        compiler_params=PARAMS,
        name="scores",
    )(occupancy, basis, high, low)


def spread_piece(terms, high, low):
    comps = terms[0].shape[0]
    on_low = dot(jnp.concatenate(terms[:2], axis=0), low, NN)
    on_high = dot(jnp.concatenate(terms, axis=0), high, NN)
    small = on_low[comps:] + on_high[2 * comps:]
    middle = on_low[:comps] + on_high[comps:2 * comps]
    return (small + middle) + on_high[:comps]


def spread_kernel(count, picks, me_ref, *refs):
    score_refs, outs = refs[:count], refs[count + 4:]
    high_ref, low_ref, sum_ref, occ_ref = refs[count:count + 4]
    scores = tree_sum([ref[...] for ref in score_refs])
    comps = scores.shape[0]
    terms = split_terms(scores, 3)
    eye = lax.broadcasted_iota(jnp.int32, (comps, LANES), 0) == lax.broadcasted_iota(jnp.int32, (comps, LANES), 1)
    row_sums = jnp.sum(jnp.where(eye, jnp.sum(scores, axis=1, keepdims=True), 0.0), axis=0, keepdims=True)
    chunks = high_ref.shape[1] // (LANES * lax.axis_size("cells"))
    width = chunks * LANES
    blocks = [(pick, out, at) for group, out in zip(picks, outs) for at, pick in enumerate(group)]
    rows = block_rows(comps, chunks)
    for pick, out, at_block in blocks:
        base = at_block * rows
        start = pl.multiple_of((me_ref[0] ^ pick) * width, width)
        lanes = pl.ds(start, width)
        piece = spread_piece(terms, high_ref[:, lanes], low_ref[:, lanes]) * occ_ref[:, lanes]
        sums = sum_ref[:, lanes] * occ_ref[:, lanes]
        extra = [row_sums]
        for at in range(chunks):
            out[base + at * comps:base + (at + 1) * comps] = piece[:, at * LANES:(at + 1) * LANES]
            extra.append(sums[:, at * LANES:(at + 1) * LANES])
        extra.append(jnp.zeros((rows - chunks * comps - chunks - 1, LANES), F32))
        out[base + chunks * comps:base + rows] = jnp.concatenate(extra, axis=0)


def block_rows(comps, chunks):
    return comps * chunks + -(-(chunks + 1) // 8) * 8


def spread_pieces(me, scores, high, low, sums, occ, picks):
    comps = scores[0].shape[0]
    chunks = high.shape[1] // (LANES * lax.axis_size("cells"))
    rows = block_rows(comps, chunks)
    count = sum(len(group) for group in picks)
    return pl.pallas_call(
        functools.partial(spread_kernel, len(scores), picks),
        out_shape=[jax.ShapeDtypeStruct((len(group) * rows, LANES), F32) for group in picks],
        in_specs=[SCALARS] + [WHOLE] * (len(scores) + 4),
        out_specs=[WHOLE] * len(picks),
        compiler_params=PARAMS,
        cost_estimate=pl.CostEstimate(
            flops=10 * comps * count * chunks * LANES * high.shape[0], bytes_accessed=2**21, transcendentals=0
        ),
        name="spread",
    )(me, *scores, high, low, sums, occ)


def gram_kernel(scale, chunks, *refs):
    pieces, (spread_ref, gram_ref) = refs[:-2], refs[-2:]
    comps = spread_ref.shape[0]
    rows = block_rows(comps, chunks)
    total = tree_sum([ref[ref.shape[0] - rows:] for ref in pieces])
    extra = total[chunks * comps:chunks * comps + chunks + 1]
    eye = lax.broadcasted_iota(jnp.int32, (comps, LANES), 0) == lax.broadcasted_iota(jnp.int32, (comps, LANES), 1)
    row_sums = jnp.sum(jnp.where(eye, extra[:1], 0.0), axis=1, keepdims=True) * scale
    parts = [total[at * comps:(at + 1) * comps] - row_sums * extra[at + 1:at + 2] for at in range(chunks)]
    spread = jnp.concatenate(parts, axis=1)
    spread_ref[...] = spread
    gram_ref[...] = packed_gram(spread)


def packed_gram(spread):
    gram = lax.dot_general(spread, spread, NT, precision=lax.Precision.HIGHEST, preferred_element_type=F32)
    half = spread.shape[0] // 2
    return jnp.concatenate([gram[:half], gram[half:]], axis=1)


def centered_gram(pieces, comps, cell_total):
    chunks = pieces[0].shape[0] // comps
    return pl.pallas_call(
        functools.partial(gram_kernel, 1.0 / cell_total, chunks),
        out_shape=(
            jax.ShapeDtypeStruct((comps, chunks * LANES), F32),
            jax.ShapeDtypeStruct((comps // 2, comps * 2), F32),
        ),
        in_specs=[WHOLE] * len(pieces),
        out_specs=(WHOLE, WHOLE),
        compiler_params=PARAMS,
        name="gram",
    )(*pieces)


def plain_gram_kernel(scale, spread_ref, row_ref, sum_ref, out_ref, gram_ref):
    spread = spread_ref[...] - row_ref[...] * scale * sum_ref[...]
    out_ref[...] = spread
    gram_ref[...] = packed_gram(spread)


def plain_gram(spread, rows, sums, cell_total):
    comps, width = spread.shape
    return pl.pallas_call(
        functools.partial(plain_gram_kernel, 1.0 / cell_total),
        out_shape=(
            jax.ShapeDtypeStruct((comps, width), F32),
            jax.ShapeDtypeStruct((comps // 2, comps * 2), F32),
        ),
        in_specs=[WHOLE] * 3,
        out_specs=(WHOLE, WHOLE),
        compiler_params=PARAMS,
        name="plain_gram",
    )(spread, rows, sums)


def row_of(x, at):
    return jnp.broadcast_to(x[at:at + 1, :], x.shape)


def spread_column(rows, at):
    return jnp.broadcast_to(rows[:, at:at + 1], rows.shape)


def eliminate(groups, begin):
    groups = list(groups)
    edge = groups[0].shape[0]
    below = lax.broadcasted_iota(jnp.int32, groups[0].shape, 0)
    columns = [{c: spread_column(rows, begin + c) for c in range(edge)} for rows in groups]
    for at in range(len(groups)):
        scale = jnp.zeros_like(groups[0])
        later = (at + 1) * edge
        for i in range(at * edge, later, 2):
            if i == later - 4 and at + 1 < len(groups):
                for rows, cols in zip(groups[at:], columns[at:]):
                    cols.update({c: spread_column(rows, begin + c) for c in range(later, later + edge)})
            row = i - at * edge
            cols = columns[at]
            first, second = cols[i], cols[i + 1]
            a, b, c = row_of(first, row), row_of(second, row), row_of(second, row + 1)
            det = a * c - b * b
            inv_a = pl.reciprocal(a, approx=True)
            inv_c = a * pl.reciprocal(det, approx=True)
            ratio = b * inv_a
            scale = jnp.where(below == row, lax.rsqrt(a), jnp.where(below == row + 1, lax.rsqrt(det * inv_a), scale))
            factors = []
            for k in cols:
                if k > i + 1:
                    top = row_of(cols[k], row)
                    factors.append((k, top * inv_a, (row_of(cols[k], row + 1) - ratio * top) * inv_c))
            rows = groups[at]
            upper = row_of(rows, row) * inv_a
            rows = rows - jnp.where(below > row, first, 0.0) * upper
            lower = row_of(rows, row + 1) * inv_c
            groups[at] = rows - jnp.where(below > row + 1, second - ratio * first, 0.0) * lower
            for ahead in range(at, len(groups)):
                cols = columns[ahead]
                first = cols[i]
                second = cols[i + 1] - ratio * first
                for k, on_first, on_second in factors:
                    cols[k] = cols[k] - first * on_first - second * on_second
                if ahead > at:
                    groups[ahead] = groups[ahead] - first * upper - second * lower
                del cols[i], cols[i + 1]
        groups[at] = groups[at] * scale
    return groups


def scale_kernel(gram_ref, times_ref, plus_ref):
    gram = gram_ref[...]
    half, comps = gram.shape[0], gram.shape[1] // 2
    gram = jnp.concatenate([gram[:, :comps], gram[:, comps:]], axis=0)
    eye = lax.broadcasted_iota(jnp.int32, gram.shape, 0) == lax.broadcasted_iota(jnp.int32, gram.shape, 1)
    diagonal = jnp.where(eye, gram, 0.0)
    row_scale = lax.rsqrt(jnp.sum(diagonal, axis=1, keepdims=True))
    col_scale = lax.rsqrt(jnp.sum(diagonal, axis=0, keepdims=True))
    zeros = jnp.zeros_like(gram)
    times_ref[...] = jnp.concatenate([zeros, row_scale * col_scale], axis=1)
    plus_ref[...] = jnp.concatenate([jnp.where(eye, col_scale, 0.0), zeros], axis=1)


def scales(gram):
    half, lanes = gram.shape
    return pl.pallas_call(
        scale_kernel,
        out_shape=[jax.ShapeDtypeStruct((2 * half, lanes), F32)] * 2,
        in_specs=[WHOLE],
        out_specs=[WHOLE, WHOLE],
        compiler_params=PARAMS,
        name="scales",
    )(gram)


def basis_kernel(scale, *refs):
    grams, (times_ref, plus_ref, spread_ref, out_ref) = refs[:-4], refs[-4:]
    gram = tree_sum([ref[...] for ref in grams])
    comps = spread_ref.shape[0]
    gram = jnp.concatenate([pltpu.roll(gram, comps, 1), gram], axis=0)
    both = gram * times_ref[...] + plus_ref[...]
    groups = eliminate([both[at:at + 8] for at in range(0, comps, 8)], comps)
    inverse = jnp.concatenate(groups, axis=0)[:, :comps] * scale
    out_ref[...] = lax.dot_general(
        inverse, spread_ref[...], NN, precision=lax.Precision.HIGHEST, preferred_element_type=F32
    )


def orthonormal(grams, spread, scale):
    return pl.pallas_call(
        functools.partial(basis_kernel, scale),
        out_shape=jax.ShapeDtypeStruct(spread.shape, F32),
        in_specs=[WHOLE] * (len(grams) + 3),
        out_specs=WHOLE,
        compiler_params=PARAMS,
        name="orthonormal",
    )(*grams, *scales(grams[0]), spread)


def send(x, offset_cells, offset_genes):
    cells, genes = lax.axis_size("cells"), lax.axis_size("genes")
    pairs = []
    for c in range(cells):
        for g in range(genes):
            pairs.append((c * genes + g, (c ^ offset_cells) * genes + (g ^ offset_genes)))
    return lax.ppermute(x, ("cells", "genes"), pairs)


def gene_terms(x):
    x = x + send(x, 0, 1)
    return [x, send(x, 0, 3)]


def all_terms(x):
    x = x + send(x, 0, 1)
    across = [send(x, c, g) for c, g in ((1, 3), (1, 1), (0, 3))]
    terms = [x + across[2], across[1] + across[0]]
    for at in range(1, lax.axis_size("cells").bit_length() - 1):
        x = tree_sum(terms)
        terms = [x, send(x, 1 << at, 1)]
    return terms


def scattered_spread(scores, high, low, sums, occ, cell_total):
    comps = scores[0].shape[0]
    me = lax.axis_index("cells").astype(jnp.int32).reshape(1)
    make = functools.partial(spread_pieces, scores=scores, high=high, low=low, sums=sums, occ=occ)
    first, second, across = make(me, picks=[[5], [6], [7]])
    first, me = lax.optimization_barrier((first, me))
    first, second = send(first, 1, 0), send(second, 2, 0)
    straight = [send(across, 7, 0)]
    far, own, *others = make(me, picks=[[4], [0], [3], [2], [1]])
    first, others[0] = lax.optimization_barrier((first, others[0]))
    far = lax.optimization_barrier(far + first) + second
    far, others[1], others[2] = lax.optimization_barrier((far, others[1], others[2]))
    straight += [send(x, k, 0) for k, x in zip((3, 2, 1), others)]
    return centered_gram([own, send(far, 4, 0)] + straight, comps, cell_total)


def all_alike(counts, occupancy, start_basis):
    tile_rows, tile_cols = occupancy.shape
    edge = counts.shape[0] // tile_rows
    logged = jnp.log(1.0 + counts.astype(F32)).reshape(tile_rows, edge, tile_cols, -1)
    logged = (logged * occupancy.astype(F32)[:, None, :, None]).reshape(counts.shape)
    high, low = split_terms(logged, 2)
    scores = lax.psum(dot(start_basis, high, NT) + dot(start_basis, low, NT), "genes")
    spread = spread_piece(split_terms(scores, 3), high, low)
    spread = lax.psum_scatter(spread, "cells", scatter_dimension=1, tiled=True)
    rows = lax.psum(jnp.sum(scores, axis=1, keepdims=True), "cells")
    sums = lax.psum_scatter(jnp.sum(logged, axis=0, keepdims=True), "cells", scatter_dimension=1, tiled=True)
    spread, gram = plain_gram(spread, rows, sums, counts.shape[0] * lax.axis_size("cells"))
    return [lax.psum(gram, ("cells", "genes"))], spread


def in_steps(counts, occupancy, start_basis):
    high, low, sums = log_terms(counts)
    scores, occ = score_part(occupancy, start_basis, high, low)
    cell_total = counts.shape[0] * lax.axis_size("cells")
    spread, gram = scattered_spread(gene_terms(scores), high, low, sums, occ, cell_total)
    return all_terms(gram), spread


def on_device(counts, occupancy, start_basis):
    gene_count = counts.shape[1]
    cells, genes = lax.axis_size("cells"), lax.axis_size("genes")
    halvings = cells == 1 << 3 and genes == 1 << 2
    tiles = occupancy.shape[0] == 1 and gene_count == occupancy.shape[1] * LANES
    work = in_steps if halvings and tiles and gene_count % (cells * LANES) == 0 else all_alike
    grams, spread = work(counts, occupancy, start_basis)
    return orthonormal(grams, spread, math.sqrt(gene_count * genes))


def solution(mesh):
    in_specs = (P("cells", "genes"), P("cells", "genes"), P(None, "genes"))
    out_specs = P(None, ("genes", "cells"))
    return jax.shard_map(
        on_device, mesh=mesh, in_specs=in_specs, out_specs=out_specs, check_vma=False
    )
```

profile of v0, /device:TPU:0, one launch (start us, length us, event | category | flops | bytes accessed | tf_op | source)
XLA Modules:
  0.0 47.6 jit_solution(9878928614286842332)
XLA Ops:
  0.0 1.9 %log_terms.1 = (bf16[128,4096]{1,0:T(8,128)(2,1)S(1)}, bf16[128,4096]{1,0:T(8,128)(2,1)S(1)}, f32[1,4096]{1,0:T(1,128)S(1)}) custom-call(bf16[128,4096]{1,0:T(8,128)(2,1)} %counts_hbm.1), custom_call_target="tpu_custom_call" | custom-call | flops 10485760 | bytes 4194304 | tf_op jit(solution)/shard_map/log_terms/pallas_call | solution.py:65
  1.9 0.6 %copy-done.1 = s32[1,32]{1,0:T(1,128)S(1)} copy-done((s32[1,32]{1,0:T(1,128)S(1)}, s32[1,32]{1,0:T(1,128)}, u32[]{:S(2)}) %copy-start.1) | copy-done | bytes 152
  2.6 0.9 %scores.1 = (f32[64,128]{1,0:T(8,128)S(1)}, f32[1,4096]{1,0:T(1,128)S(1)}) custom-call(s32[1,32]{1,0:T(1,128)S(1)} %copy-done.1, bf16[64,4096]{1,0:T(8,128)(2,1)S(1)} %copy-done, bf16[128,4096]{1,0:T(8,128)(2,1)S(1)} %get-tuple-element.29.high_ref.refs_2_, bf16[128,4096]{1,0:T(8,128)(2,1)S(1)} %get-tuple-element.30.low_ref.refs_3_), custom_call_target="tpu_custom_call" | custom-call | tf_op jit(solution)/shard_map/scores/pallas_call | solution.py:102
  4.0 0.9 %collective-permute-done = f32[64,128]{1,0:T(8,128)S(1)} collective-permute-done((f32[64,128]{1,0:T(8,128)S(1)}, f32[64,128]{1,0:T(8,128)S(1)}, u32[]{:S(2)}, u32[]{:S(2)}) %collective-permute-start) | collective-permute-done | bytes 32800 | tf_op jit(solution)/shard_map/ppermute | solution.py:332
  4.8 2.6 %collective-permute-start.1 = (f32[64,128]{1,0:T(8,128)S(1)}, f32[64,128]{1,0:T(8,128)S(1)}, u32[]{:S(2)}, u32[]{:S(2)}) collective-permute-start(f32[64,128]{1,0:T(8,128)S(1)} %add.24.refs_0_), channel_id=1, source_target_pairs={{0,3},{1,2},{2,1},{3,0},{4,7},{5,6},{6,5},{7,4},{8,11},{9,10},{10,... | collective-permute-start | bytes 98312 | tf_op jit(solution)/shard_map/ppermute | solution.py:332
  7.5 1.6 %collective-permute-done.1.refs_1_ = f32[64,128]{1,0:T(8,128)S(1)} collective-permute-done((f32[64,128]{1,0:T(8,128)S(1)}, f32[64,128]{1,0:T(8,128)S(1)}, u32[]{:S(2)}, u32[]{:S(2)}) %collective-permute-start.1) | collective-permute-done | bytes 32800 | tf_op jit(solution)/shard_map/ppermute | solution.py:332
  9.5 2.1 %collective-permute-start.2 = (f32[264,128]{1,0:T(8,128)S(1)}, f32[264,128]{1,0:T(8,128)S(1)}, u32[]{:S(2)}, u32[]{:S(2)}) collective-permute-start(f32[264,128]{1,0:T(8,128)S(1)} %get-tuple-element.38), channel_id=1, source_target_pairs={{0,4},{1,5},{2,6},{3,7},{4,0},{5,1},{6,2},{7,3},{8,12},{9,13},{10,... | collective-permute-start | bytes 405512 | tf_op jit(solution)/shard_map/ppermute | solution.py:332
  11.5 1.6 %collective-permute-start.3 = (f32[264,128]{1,0:T(8,128)S(1)}, f32[264,128]{1,0:T(8,128)S(1)}, u32[]{:S(2)}, u32[]{:S(2)}) collective-permute-start(f32[264,128]{1,0:T(8,128)S(1)} %get-tuple-element.41), channel_id=1, source_target_pairs={{0,8},{1,9},{2,10},{3,11},{4,12},{5,13},{6,14},{7,15},{8,0},{9,1},... | collective-permute-start | bytes 405512 | tf_op jit(solution)/shard_map/ppermute | solution.py:332
  13.1 2.4 %collective-permute-start.5 = (f32[264,128]{1,0:T(8,128)S(1)}, f32[264,128]{1,0:T(8,128)S(1)}, u32[]{:S(2)}, u32[]{:S(2)}) collective-permute-start(f32[264,128]{1,0:T(8,128)S(1)} %get-tuple-element.45), channel_id=1, source_target_pairs={{0,28},{1,29},{2,30},{3,31},{4,24},{5,25},{6,26},{7,27},{8,20},{9,... | collective-permute-start | bytes 405512 | tf_op jit(solution)/shard_map/ppermute | solution.py:332
  15.5 0.6 %spread.3 = (f32[264,128]{1,0:T(8,128)S(1)}, f32[264,128]{1,0:T(8,128)S(1)}, f32[264,128]{1,0:T(8,128)S(1)}, f32[264,128]{1,0:T(8,128)S(1)}, f32[264,128]{1,0:T(8,128)S(1)}) custom-call(s32[1]{0:T(128)} %bitcast.me_ref, f32[64,128]{1,0:T(8,128)S(1)} %add.24.refs_0_, f32[64,128]{1,0:T(8,128)S(1)} %collective-permute-done.1.refs_1_, ...), custom_call_target="tpu_custom_call" | custom-call | flops 209715200 | bytes 2097152 | tf_op jit(solution)/shard_map/spread/pallas_call | solution.py:156
  16.2 4.3 %collective-permute-start.6 = (f32[264,128]{1,0:T(8,128)S(1)}, f32[264,128]{1,0:T(8,128)S(1)}, u32[]{:S(2)}, u32[]{:S(2)}) collective-permute-start(f32[264,128]{1,0:T(8,128)S(1)} %get-tuple-element.46), channel_id=1, source_target_pairs={{0,12},{1,13},{2,14},{3,15},{4,8},{5,9},{6,10},{7,11},{8,4},{9,5},... | collective-permute-start | bytes 405512 | tf_op jit(solution)/shard_map/ppermute | solution.py:332
  21.0 2.5 %collective-permute-start.7 = (f32[264,128]{1,0:T(8,128)S(1)}, f32[264,128]{1,0:T(8,128)S(1)}, u32[]{:S(2)}, u32[]{:S(2)}) collective-permute-start(f32[264,128]{1,0:T(8,128)S(1)} %get-tuple-element.47), channel_id=1, source_target_pairs={{0,8},{1,9},{2,10},{3,11},{4,12},{5,13},{6,14},{7,15},{8,0},{9,1},... | collective-permute-start | bytes 405512 | tf_op jit(solution)/shard_map/ppermute | solution.py:332
  23.5 3.2 %collective-permute-done.6.refs_3_ = f32[264,128]{1,0:T(8,128)S(1)} collective-permute-done((f32[264,128]{1,0:T(8,128)S(1)}, f32[264,128]{1,0:T(8,128)S(1)}, u32[]{:S(2)}, u32[]{:S(2)}) %collective-permute-start.6) | collective-permute-done | bytes 135200 | tf_op jit(solution)/shard_map/ppermute | solution.py:332
  27.2 2.8 %collective-permute-done.7.refs_4_ = f32[264,128]{1,0:T(8,128)S(1)} collective-permute-done((f32[264,128]{1,0:T(8,128)S(1)}, f32[264,128]{1,0:T(8,128)S(1)}, u32[]{:S(2)}, u32[]{:S(2)}) %collective-permute-start.7) | collective-permute-done | bytes 135200 | tf_op jit(solution)/shard_map/ppermute | solution.py:332
  30.5 1.2 %collective-permute-done.9 = f32[32,128]{1,0:T(8,128)S(1)} collective-permute-done((f32[32,128]{1,0:T(8,128)S(1)}, f32[32,128]{1,0:T(8,128)S(1)}, u32[]{:S(2)}, u32[]{:S(2)}) %collective-permute-start.9) | collective-permute-done | bytes 16416 | tf_op jit(solution)/shard_map/ppermute | solution.py:332
  31.7 1.4 %collective-permute-start.12 = (f32[32,128]{1,0:T(8,128)S(1)}, f32[32,128]{1,0:T(8,128)S(1)}, u32[]{:S(2)}, u32[]{:S(2)}) collective-permute-start(f32[32,128]{1,0:T(8,128)S(1)} %add.27), channel_id=1, source_target_pairs={{0,7},{1,6},{2,5},{3,4},{4,3},{5,2},{6,1},{7,0},{8,15},{9,14},{10,... | collective-permute-start | bytes 49160 | tf_op jit(solution)/shard_map/ppermute | solution.py:332
  33.0 1.3 %collective-permute-start.11 = (f32[32,128]{1,0:T(8,128)S(1)}, f32[32,128]{1,0:T(8,128)S(1)}, u32[]{:S(2)}, u32[]{:S(2)}) collective-permute-start(f32[32,128]{1,0:T(8,128)S(1)} %add.27), channel_id=1, source_target_pairs={{0,5},{1,4},{2,7},{3,6},{4,1},{5,0},{6,3},{7,2},{8,13},{9,12},{10,... | collective-permute-start | bytes 49160 | tf_op jit(solution)/shard_map/ppermute | solution.py:332
  34.7 1.1 %collective-permute-done.12 = f32[32,128]{1,0:T(8,128)S(1)} collective-permute-done((f32[32,128]{1,0:T(8,128)S(1)}, f32[32,128]{1,0:T(8,128)S(1)}, u32[]{:S(2)}, u32[]{:S(2)}) %collective-permute-start.12) | collective-permute-done | bytes 16416 | tf_op jit(solution)/shard_map/ppermute | solution.py:332
  35.7 0.5 %collective-permute-done.11 = f32[32,128]{1,0:T(8,128)S(1)} collective-permute-done((f32[32,128]{1,0:T(8,128)S(1)}, f32[32,128]{1,0:T(8,128)S(1)}, u32[]{:S(2)}, u32[]{:S(2)}) %collective-permute-start.11) | collective-permute-done | bytes 16416 | tf_op jit(solution)/shard_map/ppermute | solution.py:332
  36.3 1.3 %collective-permute-done.10 = f32[32,128]{1,0:T(8,128)S(1)} collective-permute-done((f32[32,128]{1,0:T(8,128)S(1)}, f32[32,128]{1,0:T(8,128)S(1)}, u32[]{:S(2)}, u32[]{:S(2)}) %collective-permute-start.10) | collective-permute-done | bytes 16416 | tf_op jit(solution)/shard_map/ppermute | solution.py:332
  37.6 3.2 %collective-permute-done.13 = f32[32,128]{1,0:T(8,128)S(1)} collective-permute-done((f32[32,128]{1,0:T(8,128)S(1)}, f32[32,128]{1,0:T(8,128)S(1)}, u32[]{:S(2)}, u32[]{:S(2)}) %collective-permute-start.13) | collective-permute-done | bytes 16416 | tf_op jit(solution)/shard_map/ppermute | solution.py:332
  40.8 0.8 %collective-permute-start.14 = (f32[32,128]{1,0:T(8,128)S(1)}, f32[32,128]{1,0:T(8,128)S(1)}, u32[]{:S(2)}, u32[]{:S(2)}) collective-permute-start(f32[32,128]{1,0:T(8,128)S(1)} %add.31.gram_ref.refs_0_), channel_id=1, source_target_pairs={{0,17},{1,16},{2,19},{3,18},{4,21},{5,20},{6,23},{7,22},{8,25},{9,... | collective-permute-start | bytes 49160 | tf_op jit(solution)/shard_map/ppermute | solution.py:332
  41.8 3.2 %collective-permute-done.14.refs_1_ = f32[32,128]{1,0:T(8,128)S(1)} collective-permute-done((f32[32,128]{1,0:T(8,128)S(1)}, f32[32,128]{1,0:T(8,128)S(1)}, u32[]{:S(2)}, u32[]{:S(2)}) %collective-permute-start.14) | collective-permute-done | bytes 16416 | tf_op jit(solution)/shard_map/ppermute | solution.py:332
  45.0 2.6 %orthonormal.1 = f32[64,512]{1,0:T(8,128)} custom-call(f32[32,128]{1,0:T(8,128)S(1)} %add.31.gram_ref.refs_0_, f32[32,128]{1,0:T(8,128)S(1)} %collective-permute-done.14.refs_1_, f32[64,128]{1,0:T(8,128)S(1)} %get-tuple-element.50.refs_2_, f32[64,128]{1,0:T(8,128)S(1)} %get-tuple-element.51.refs_3_, f32[64,512]{1,0:T(8,128)S(1)} %get-tuple-element.52.refs_4_), custom_call_target="tpu_custom_call" | custom-call | tf_op jit(solution)/shard_map/orthonormal/pallas_call | solution.py:316
  (23 shorter events, 3.0 us)
Async XLA Ops:
  0.0 1.9 %copy-start = (bf16[64,4096]{1,0:T(8,128)(2,1)S(1)}, bf16[64,4096]{1,0:T(8,128)(2,1)}, u32[]{:S(2)}) copy-start(bf16[64,4096]{1,0:T(8,128)(2,1)} %basis_ref.1) | copy-start | bytes 1572868
  1.9 0.7 %copy-start.1 = (s32[1,32]{1,0:T(1,128)S(1)}, s32[1,32]{1,0:T(1,128)}, u32[]{:S(2)}) copy-start(s32[1,32]{1,0:T(1,128)} %occ_ref.1) | copy-start | bytes 388
  3.5 1.4 %collective-permute-start = (f32[64,128]{1,0:T(8,128)S(1)}, f32[64,128]{1,0:T(8,128)S(1)}, u32[]{:S(2)}, u32[]{:S(2)}) collective-permute-start(f32[64,128]{1,0:T(8,128)S(1)} %get-tuple-element.31), channel_id=1, source_target_pairs={{0,1},{1,0},{2,3},{3,2},{4,5},{5,4},{6,7},{7,6},{8,9},{9,8},{10,11... | collective-permute-start | bytes 98312 | tf_op jit(solution)/shard_map/ppermute | solution.py:332
  4.8 4.2 %collective-permute-start.1 = (f32[64,128]{1,0:T(8,128)S(1)}, f32[64,128]{1,0:T(8,128)S(1)}, u32[]{:S(2)}, u32[]{:S(2)}) collective-permute-start(f32[64,128]{1,0:T(8,128)S(1)} %add.24.refs_0_), channel_id=1, source_target_pairs={{0,3},{1,2},{2,1},{3,0},{4,7},{5,6},{6,5},{7,4},{8,11},{9,10},{10,... | collective-permute-start | bytes 98312 | tf_op jit(solution)/shard_map/ppermute | solution.py:332
  9.5 6.7 %collective-permute-start.2 = (f32[264,128]{1,0:T(8,128)S(1)}, f32[264,128]{1,0:T(8,128)S(1)}, u32[]{:S(2)}, u32[]{:S(2)}) collective-permute-start(f32[264,128]{1,0:T(8,128)S(1)} %get-tuple-element.38), channel_id=1, source_target_pairs={{0,4},{1,5},{2,6},{3,7},{4,0},{5,1},{6,2},{7,3},{8,12},{9,13},{10,... | collective-permute-start | bytes 405512 | tf_op jit(solution)/shard_map/ppermute | solution.py:332
  11.5 8.9 %collective-permute-start.3 = (f32[264,128]{1,0:T(8,128)S(1)}, f32[264,128]{1,0:T(8,128)S(1)}, u32[]{:S(2)}, u32[]{:S(2)}) collective-permute-start(f32[264,128]{1,0:T(8,128)S(1)} %get-tuple-element.41), channel_id=1, source_target_pairs={{0,8},{1,9},{2,10},{3,11},{4,12},{5,13},{6,14},{7,15},{8,0},{9,1},... | collective-permute-start | bytes 405512 | tf_op jit(solution)/shard_map/ppermute | solution.py:332
  13.1 10.4 %collective-permute-start.5 = (f32[264,128]{1,0:T(8,128)S(1)}, f32[264,128]{1,0:T(8,128)S(1)}, u32[]{:S(2)}, u32[]{:S(2)}) collective-permute-start(f32[264,128]{1,0:T(8,128)S(1)} %get-tuple-element.45), channel_id=1, source_target_pairs={{0,28},{1,29},{2,30},{3,31},{4,24},{5,25},{6,26},{7,27},{8,20},{9,... | collective-permute-start | bytes 405512 | tf_op jit(solution)/shard_map/ppermute | solution.py:332
  16.2 10.5 %collective-permute-start.6 = (f32[264,128]{1,0:T(8,128)S(1)}, f32[264,128]{1,0:T(8,128)S(1)}, u32[]{:S(2)}, u32[]{:S(2)}) collective-permute-start(f32[264,128]{1,0:T(8,128)S(1)} %get-tuple-element.46), channel_id=1, source_target_pairs={{0,12},{1,13},{2,14},{3,15},{4,8},{5,9},{6,10},{7,11},{8,4},{9,5},... | collective-permute-start | bytes 405512 | tf_op jit(solution)/shard_map/ppermute | solution.py:332
  20.5 6.7 %collective-permute-start.4 = (f32[264,128]{1,0:T(8,128)S(1)}, f32[264,128]{1,0:T(8,128)S(1)}, u32[]{:S(2)}, u32[]{:S(2)}) collective-permute-start(f32[264,128]{1,0:T(8,128)S(1)} %add.26), channel_id=1, source_target_pairs={{0,16},{1,17},{2,18},{3,19},{4,20},{5,21},{6,22},{7,23},{8,24},{9,... | collective-permute-start | bytes 405512 | tf_op jit(solution)/shard_map/ppermute | solution.py:332
  21.0 9.1 %collective-permute-start.7 = (f32[264,128]{1,0:T(8,128)S(1)}, f32[264,128]{1,0:T(8,128)S(1)}, u32[]{:S(2)}, u32[]{:S(2)}) collective-permute-start(f32[264,128]{1,0:T(8,128)S(1)} %get-tuple-element.47), channel_id=1, source_target_pairs={{0,8},{1,9},{2,10},{3,11},{4,12},{5,13},{6,14},{7,15},{8,0},{9,1},... | collective-permute-start | bytes 405512 | tf_op jit(solution)/shard_map/ppermute | solution.py:332
  23.5 6.6 %collective-permute-start.8 = (f32[264,128]{1,0:T(8,128)S(1)}, f32[264,128]{1,0:T(8,128)S(1)}, u32[]{:S(2)}, u32[]{:S(2)}) collective-permute-start(f32[264,128]{1,0:T(8,128)S(1)} %get-tuple-element.48), channel_id=1, source_target_pairs={{0,4},{1,5},{2,6},{3,7},{4,0},{5,1},{6,2},{7,3},{8,12},{9,13},{10,... | collective-permute-start | bytes 405512 | tf_op jit(solution)/shard_map/ppermute | solution.py:332
  30.5 1.2 %collective-permute-start.9 = (f32[32,128]{1,0:T(8,128)S(1)}, f32[32,128]{1,0:T(8,128)S(1)}, u32[]{:S(2)}, u32[]{:S(2)}) collective-permute-start(f32[32,128]{1,0:T(8,128)S(1)} %get-tuple-element.49), channel_id=1, source_target_pairs={{0,1},{1,0},{2,3},{3,2},{4,5},{5,4},{6,7},{7,6},{8,9},{9,8},{10,11... | collective-permute-start | bytes 49160 | tf_op jit(solution)/shard_map/ppermute | solution.py:332
  31.7 4.1 %collective-permute-start.12 = (f32[32,128]{1,0:T(8,128)S(1)}, f32[32,128]{1,0:T(8,128)S(1)}, u32[]{:S(2)}, u32[]{:S(2)}) collective-permute-start(f32[32,128]{1,0:T(8,128)S(1)} %add.27), channel_id=1, source_target_pairs={{0,7},{1,6},{2,5},{3,4},{4,3},{5,2},{6,1},{7,0},{8,15},{9,14},{10,... | collective-permute-start | bytes 49160 | tf_op jit(solution)/shard_map/ppermute | solution.py:332
  33.0 3.2 %collective-permute-start.11 = (f32[32,128]{1,0:T(8,128)S(1)}, f32[32,128]{1,0:T(8,128)S(1)}, u32[]{:S(2)}, u32[]{:S(2)}) collective-permute-start(f32[32,128]{1,0:T(8,128)S(1)} %add.27), channel_id=1, source_target_pairs={{0,5},{1,4},{2,7},{3,6},{4,1},{5,0},{6,3},{7,2},{8,13},{9,12},{10,... | collective-permute-start | bytes 49160 | tf_op jit(solution)/shard_map/ppermute | solution.py:332
  34.4 3.2 %collective-permute-start.10 = (f32[32,128]{1,0:T(8,128)S(1)}, f32[32,128]{1,0:T(8,128)S(1)}, u32[]{:S(2)}, u32[]{:S(2)}) collective-permute-start(f32[32,128]{1,0:T(8,128)S(1)} %add.27), channel_id=1, source_target_pairs={{0,3},{1,2},{2,1},{3,0},{4,7},{5,6},{6,5},{7,4},{8,11},{9,10},{10,... | collective-permute-start | bytes 49160 | tf_op jit(solution)/shard_map/ppermute | solution.py:332
  37.5 3.2 %collective-permute-start.13 = (f32[32,128]{1,0:T(8,128)S(1)}, f32[32,128]{1,0:T(8,128)S(1)}, u32[]{:S(2)}, u32[]{:S(2)}) collective-permute-start(f32[32,128]{1,0:T(8,128)S(1)} %add_add_fusion), channel_id=1, source_target_pairs={{0,9},{1,8},{2,11},{3,10},{4,13},{5,12},{6,15},{7,14},{8,1},{9,0},... | collective-permute-start | bytes 49160 | tf_op jit(solution)/shard_map/ppermute | solution.py:332
  40.8 4.2 %collective-permute-start.14 = (f32[32,128]{1,0:T(8,128)S(1)}, f32[32,128]{1,0:T(8,128)S(1)}, u32[]{:S(2)}, u32[]{:S(2)}) collective-permute-start(f32[32,128]{1,0:T(8,128)S(1)} %add.31.gram_ref.refs_0_), channel_id=1, source_target_pairs={{0,17},{1,16},{2,19},{3,18},{4,21},{5,20},{6,23},{7,22},{8,25},{9,... | collective-permute-start | bytes 49160 | tf_op jit(solution)/shard_map/ppermute | solution.py:332
where the time goes:
time: 47.7 us; the launch traced here: 47.6 us
  starting transfers between devices  20.4 us (43%)
  waiting for transfers between devices  19.4 us (41%)
  Pallas kernels  6.99 us (15%)
  local copies, waits for them, and re-layouts  0.64 us (1%)
    ppermute x15, starting transfers between devices, send(): return lax.ppermute(x, ('cells', 'genes'), pairs)  20.4 us
    ppermute x15, waiting for transfers between devices, send(): return lax.ppermute(x, ('cells', 'genes'), pairs)  19.4 us
    pallas_call x1, Pallas kernels, orthonormal(): pl.pallas_call(functools.partial(basis_kernel, scale), out_shape=jax.Shap...  2.58 us
    pallas_call x1, Pallas kernels, log_terms(): pl.pallas_call(functools.partial(log_kernel, width), out_shape=(jax.Shape...  1.92 us
    pallas_call x2, Pallas kernels, spread_pieces(): pl.pallas_call(functools.partial(spread_kernel, len(scores), picks), out_...  0.99 us
  transfers between devices with their start and end apart: 15, of which 11 were waited for; matrix products, arithmetic and copies ran while one was open for 0% of the time, Pallas kernels for 2%

commit v1 on v0

--- a/solution.py
+++ b/solution.py
@@ -351,15 +351,14 @@
     comps = scores[0].shape[0]
     me = lax.axis_index("cells").astype(jnp.int32).reshape(1)
     make = functools.partial(spread_pieces, scores=scores, high=high, low=low, sums=sums, occ=occ)
-    first, second, across = make(me, picks=[[5], [6], [7]])
+    first, second, near, across = make(me, picks=[[5], [6], [2], [7]])
     first, me = lax.optimization_barrier((first, me))
     first, second = send(first, 1, 0), send(second, 2, 0)
-    straight = [send(across, 7, 0)]
-    far, own, *others = make(me, picks=[[4], [0], [3], [2], [1]])
-    first, others[0] = lax.optimization_barrier((first, others[0]))
+    straight = [send(near, 2, 0), send(across, 7, 0)]
+    far, own, *others = make(me, picks=[[4], [0], [3], [1]])
     far = lax.optimization_barrier(far + first) + second
-    far, others[1], others[2] = lax.optimization_barrier((far, others[1], others[2]))
-    straight += [send(x, k, 0) for k, x in zip((3, 2, 1), others)]
+    far, others = lax.optimization_barrier((far, others))
+    straight += [send(x, k, 0) for k, x in zip((3, 1), others)]
     return centered_gram([own, send(far, 4, 0)] + straight, comps, cell_total)
 
 

time: 47.7 us -> 47.8 us (level)
  starting transfers between devices: 20.4 us -> 21.6 us
  waiting for transfers between devices: 19.4 us -> 18.2 us
    ppermute x15, starting transfers between devices: 20.4 us -> 21.6 us  [send(): return lax.ppermute(x, ('cells', 'genes'), pairs)]
    ppermute x15, waiting for transfers between devices: 19.4 us -> 18.2 us  [send(): return lax.ppermute(x, ('cells', 'genes'), pairs)]
  transfers between devices with their start and end apart: 15 -> 15, of which waited for: 11 -> 12; matrix products, arithmetic and copies ran while one was open for 0% -> 0% of each run, Pallas kernels for 2% -> 1%
where the time goes in v1:
time: 47.8 us; the launch traced here: 47.6 us
  starting transfers between devices  21.6 us (45%)
  waiting for transfers between devices  18.2 us (38%)
  Pallas kernels  6.96 us (15%)
  local copies, waits for them, and re-layouts  0.64 us (1%)
    ppermute x15, starting transfers between devices, send(): return lax.ppermute(x, ('cells', 'genes'), pairs)  21.6 us
    ppermute x15, waiting for transfers between devices, send(): return lax.ppermute(x, ('cells', 'genes'), pairs)  18.2 us
    pallas_call x1, Pallas kernels, orthonormal(): pl.pallas_call(functools.partial(basis_kernel, scale), out_shape=jax.Shap...  2.57 us
    pallas_call x1, Pallas kernels, log_terms(): pl.pallas_call(functools.partial(log_kernel, width), out_shape=(jax.Shape...  1.92 us
    pallas_call x2, Pallas kernels, spread_pieces(): pl.pallas_call(functools.partial(spread_kernel, len(scores), picks), out_...  0.97 us
  transfers between devices with their start and end apart: 15, of which 12 were waited for; matrix products, arithmetic and copies ran while one was open for 0% of the time, Pallas kernels for 1%

profile of v1, /device:TPU:0, one launch (start us, length us, event | category | flops | bytes accessed | tf_op | source)
XLA Modules:
  0.0 47.6 jit_solution(13394392991167416352)
XLA Ops:
  0.0 1.9 %log_terms.1 = (bf16[128,4096]{1,0:T(8,128)(2,1)S(1)}, bf16[128,4096]{1,0:T(8,128)(2,1)S(1)}, f32[1,4096]{1,0:T(1,128)S(1)}) custom-call(bf16[128,4096]{1,0:T(8,128)(2,1)} %counts_hbm.1), custom_call_target="tpu_custom_call" | custom-call | flops 10485760 | bytes 4194304 | tf_op jit(solution)/shard_map/log_terms/pallas_call | solution.py:65
  1.9 0.6 %copy-done.1 = s32[1,32]{1,0:T(1,128)S(1)} copy-done((s32[1,32]{1,0:T(1,128)S(1)}, s32[1,32]{1,0:T(1,128)}, u32[]{:S(2)}) %copy-start.1) | copy-done | bytes 152
  2.6 0.9 %scores.1 = (f32[64,128]{1,0:T(8,128)S(1)}, f32[1,4096]{1,0:T(1,128)S(1)}) custom-call(s32[1,32]{1,0:T(1,128)S(1)} %copy-done.1, bf16[64,4096]{1,0:T(8,128)(2,1)S(1)} %copy-done, bf16[128,4096]{1,0:T(8,128)(2,1)S(1)} %get-tuple-element.27.high_ref.refs_2_, bf16[128,4096]{1,0:T(8,128)(2,1)S(1)} %get-tuple-element.28.low_ref.refs_3_), custom_call_target="tpu_custom_call" | custom-call | tf_op jit(solution)/shard_map/scores/pallas_call | solution.py:102
  4.0 0.9 %collective-permute-done = f32[64,128]{1,0:T(8,128)S(1)} collective-permute-done((f32[64,128]{1,0:T(8,128)S(1)}, f32[64,128]{1,0:T(8,128)S(1)}, u32[]{:S(2)}, u32[]{:S(2)}) %collective-permute-start) | collective-permute-done | bytes 32800 | tf_op jit(solution)/shard_map/ppermute | solution.py:332
  4.8 2.6 %collective-permute-start.1 = (f32[64,128]{1,0:T(8,128)S(1)}, f32[64,128]{1,0:T(8,128)S(1)}, u32[]{:S(2)}, u32[]{:S(2)}) collective-permute-start(f32[64,128]{1,0:T(8,128)S(1)} %add.24.refs_0_), channel_id=1, source_target_pairs={{0,3},{1,2},{2,1},{3,0},{4,7},{5,6},{6,5},{7,4},{8,11},{9,10},{10,... | collective-permute-start | bytes 98312 | tf_op jit(solution)/shard_map/ppermute | solution.py:332
  7.5 1.6 %collective-permute-done.1.refs_1_ = f32[64,128]{1,0:T(8,128)S(1)} collective-permute-done((f32[64,128]{1,0:T(8,128)S(1)}, f32[64,128]{1,0:T(8,128)S(1)}, u32[]{:S(2)}, u32[]{:S(2)}) %collective-permute-start.1) | collective-permute-done | bytes 32800 | tf_op jit(solution)/shard_map/ppermute | solution.py:332
  9.5 2.1 %collective-permute-start.2 = (f32[264,128]{1,0:T(8,128)S(1)}, f32[264,128]{1,0:T(8,128)S(1)}, u32[]{:S(2)}, u32[]{:S(2)}) collective-permute-start(f32[264,128]{1,0:T(8,128)S(1)} %get-tuple-element.36), channel_id=1, source_target_pairs={{0,4},{1,5},{2,6},{3,7},{4,0},{5,1},{6,2},{7,3},{8,12},{9,13},{10,... | collective-permute-start | bytes 405512 | tf_op jit(solution)/shard_map/ppermute | solution.py:332
  11.6 1.6 %collective-permute-start.3 = (f32[264,128]{1,0:T(8,128)S(1)}, f32[264,128]{1,0:T(8,128)S(1)}, u32[]{:S(2)}, u32[]{:S(2)}) collective-permute-start(f32[264,128]{1,0:T(8,128)S(1)} %get-tuple-element.37), channel_id=1, source_target_pairs={{0,8},{1,9},{2,10},{3,11},{4,12},{5,13},{6,14},{7,15},{8,0},{9,1},... | collective-permute-start | bytes 405512 | tf_op jit(solution)/shard_map/ppermute | solution.py:332
  13.6 3.5 %collective-permute-start.6 = (f32[264,128]{1,0:T(8,128)S(1)}, f32[264,128]{1,0:T(8,128)S(1)}, u32[]{:S(2)}, u32[]{:S(2)}) collective-permute-start(f32[264,128]{1,0:T(8,128)S(1)} %get-tuple-element.42), channel_id=1, source_target_pairs={{0,28},{1,29},{2,30},{3,31},{4,24},{5,25},{6,26},{7,27},{8,20},{9,... | collective-permute-start | bytes 405512 | tf_op jit(solution)/shard_map/ppermute | solution.py:332
  18.1 2.7 %collective-permute-start.4 = (f32[264,128]{1,0:T(8,128)S(1)}, f32[264,128]{1,0:T(8,128)S(1)}, u32[]{:S(2)}, u32[]{:S(2)}) collective-permute-start(f32[264,128]{1,0:T(8,128)S(1)} %add.26), channel_id=1, source_target_pairs={{0,16},{1,17},{2,18},{3,19},{4,20},{5,21},{6,22},{7,23},{8,24},{9,... | collective-permute-start | bytes 405512 | tf_op jit(solution)/shard_map/ppermute | solution.py:332
  20.8 1.5 %collective-permute-start.7 = (f32[264,128]{1,0:T(8,128)S(1)}, f32[264,128]{1,0:T(8,128)S(1)}, u32[]{:S(2)}, u32[]{:S(2)}) collective-permute-start(f32[264,128]{1,0:T(8,128)S(1)} %get-tuple-element.43), channel_id=1, source_target_pairs={{0,12},{1,13},{2,14},{3,15},{4,8},{5,9},{6,10},{7,11},{8,4},{9,5},... | collective-permute-start | bytes 405512 | tf_op jit(solution)/shard_map/ppermute | solution.py:332
  22.3 1.5 %collective-permute-start.8 = (f32[264,128]{1,0:T(8,128)S(1)}, f32[264,128]{1,0:T(8,128)S(1)}, u32[]{:S(2)}, u32[]{:S(2)}) collective-permute-start(f32[264,128]{1,0:T(8,128)S(1)} %get-tuple-element.44), channel_id=1, source_target_pairs={{0,4},{1,5},{2,6},{3,7},{4,0},{5,1},{6,2},{7,3},{8,12},{9,13},{10,... | collective-permute-start | bytes 405512 | tf_op jit(solution)/shard_map/ppermute | solution.py:332
  23.8 2.2 %collective-permute-done.6.refs_3_ = f32[264,128]{1,0:T(8,128)S(1)} collective-permute-done((f32[264,128]{1,0:T(8,128)S(1)}, f32[264,128]{1,0:T(8,128)S(1)}, u32[]{:S(2)}, u32[]{:S(2)}) %collective-permute-start.6) | collective-permute-done | bytes 135200 | tf_op jit(solution)/shard_map/ppermute | solution.py:332
  26.0 3.0 %collective-permute-done.4.refs_1_ = f32[264,128]{1,0:T(8,128)S(1)} collective-permute-done((f32[264,128]{1,0:T(8,128)S(1)}, f32[264,128]{1,0:T(8,128)S(1)}, u32[]{:S(2)}, u32[]{:S(2)}) %collective-permute-start.4) | collective-permute-done | bytes 135200 | tf_op jit(solution)/shard_map/ppermute | solution.py:332
  29.1 1.1 %collective-permute-done.8.refs_5_ = f32[264,128]{1,0:T(8,128)S(1)} collective-permute-done((f32[264,128]{1,0:T(8,128)S(1)}, f32[264,128]{1,0:T(8,128)S(1)}, u32[]{:S(2)}, u32[]{:S(2)}) %collective-permute-start.8) | collective-permute-done | bytes 135200 | tf_op jit(solution)/shard_map/ppermute | solution.py:332
  30.7 1.2 %collective-permute-done.9 = f32[32,128]{1,0:T(8,128)S(1)} collective-permute-done((f32[32,128]{1,0:T(8,128)S(1)}, f32[32,128]{1,0:T(8,128)S(1)}, u32[]{:S(2)}, u32[]{:S(2)}) %collective-permute-start.9) | collective-permute-done | bytes 16416 | tf_op jit(solution)/shard_map/ppermute | solution.py:332
  31.8 2.1 %collective-permute-start.12 = (f32[32,128]{1,0:T(8,128)S(1)}, f32[32,128]{1,0:T(8,128)S(1)}, u32[]{:S(2)}, u32[]{:S(2)}) collective-permute-start(f32[32,128]{1,0:T(8,128)S(1)} %add.27), channel_id=1, source_target_pairs={{0,7},{1,6},{2,5},{3,4},{4,3},{5,2},{6,1},{7,0},{8,15},{9,14},{10,... | collective-permute-start | bytes 49160 | tf_op jit(solution)/shard_map/ppermute | solution.py:332
  34.8 1.1 %collective-permute-done.12 = f32[32,128]{1,0:T(8,128)S(1)} collective-permute-done((f32[32,128]{1,0:T(8,128)S(1)}, f32[32,128]{1,0:T(8,128)S(1)}, u32[]{:S(2)}, u32[]{:S(2)}) %collective-permute-start.12) | collective-permute-done | bytes 16416 | tf_op jit(solution)/shard_map/ppermute | solution.py:332
  35.9 1.2 %collective-permute-done.11 = f32[32,128]{1,0:T(8,128)S(1)} collective-permute-done((f32[32,128]{1,0:T(8,128)S(1)}, f32[32,128]{1,0:T(8,128)S(1)}, u32[]{:S(2)}, u32[]{:S(2)}) %collective-permute-start.11) | collective-permute-done | bytes 16416 | tf_op jit(solution)/shard_map/ppermute | solution.py:332
  37.7 0.7 %collective-permute-start.13 = (f32[32,128]{1,0:T(8,128)S(1)}, f32[32,128]{1,0:T(8,128)S(1)}, u32[]{:S(2)}, u32[]{:S(2)}) collective-permute-start(f32[32,128]{1,0:T(8,128)S(1)} %add_add_fusion), channel_id=1, source_target_pairs={{0,9},{1,8},{2,11},{3,10},{4,13},{5,12},{6,15},{7,14},{8,1},{9,0},... | collective-permute-start | bytes 49160 | tf_op jit(solution)/shard_map/ppermute | solution.py:332
  38.4 2.5 %collective-permute-done.13 = f32[32,128]{1,0:T(8,128)S(1)} collective-permute-done((f32[32,128]{1,0:T(8,128)S(1)}, f32[32,128]{1,0:T(8,128)S(1)}, u32[]{:S(2)}, u32[]{:S(2)}) %collective-permute-start.13) | collective-permute-done | bytes 16416 | tf_op jit(solution)/shard_map/ppermute | solution.py:332
  40.9 1.4 %collective-permute-start.14 = (f32[32,128]{1,0:T(8,128)S(1)}, f32[32,128]{1,0:T(8,128)S(1)}, u32[]{:S(2)}, u32[]{:S(2)}) collective-permute-start(f32[32,128]{1,0:T(8,128)S(1)} %add.31.gram_ref.refs_0_), channel_id=1, source_target_pairs={{0,17},{1,16},{2,19},{3,18},{4,21},{5,20},{6,23},{7,22},{8,25},{9,... | collective-permute-start | bytes 49160 | tf_op jit(solution)/shard_map/ppermute | solution.py:332
  42.5 2.5 %collective-permute-done.14.refs_1_ = f32[32,128]{1,0:T(8,128)S(1)} collective-permute-done((f32[32,128]{1,0:T(8,128)S(1)}, f32[32,128]{1,0:T(8,128)S(1)}, u32[]{:S(2)}, u32[]{:S(2)}) %collective-permute-start.14) | collective-permute-done | bytes 16416 | tf_op jit(solution)/shard_map/ppermute | solution.py:332
  45.0 2.6 %orthonormal.1 = f32[64,512]{1,0:T(8,128)} custom-call(f32[32,128]{1,0:T(8,128)S(1)} %add.31.gram_ref.refs_0_, f32[32,128]{1,0:T(8,128)S(1)} %collective-permute-done.14.refs_1_, f32[64,128]{1,0:T(8,128)S(1)} %get-tuple-element.46.refs_2_, f32[64,128]{1,0:T(8,128)S(1)} %get-tuple-element.47.refs_3_, f32[64,512]{1,0:T(8,128)S(1)} %get-tuple-element.48.refs_4_), custom_call_target="tpu_custom_call" | custom-call | tf_op jit(solution)/shard_map/orthonormal/pallas_call | solution.py:316
  (23 shorter events, 4.4 us)
Async XLA Ops:
  0.0 1.9 %copy-start = (bf16[64,4096]{1,0:T(8,128)(2,1)S(1)}, bf16[64,4096]{1,0:T(8,128)(2,1)}, u32[]{:S(2)}) copy-start(bf16[64,4096]{1,0:T(8,128)(2,1)} %basis_ref.1) | copy-start | bytes 1572868
  1.9 0.7 %copy-start.1 = (s32[1,32]{1,0:T(1,128)S(1)}, s32[1,32]{1,0:T(1,128)}, u32[]{:S(2)}) copy-start(s32[1,32]{1,0:T(1,128)} %occ_ref.1) | copy-start | bytes 388
  3.5 1.4 %collective-permute-start = (f32[64,128]{1,0:T(8,128)S(1)}, f32[64,128]{1,0:T(8,128)S(1)}, u32[]{:S(2)}, u32[]{:S(2)}) collective-permute-start(f32[64,128]{1,0:T(8,128)S(1)} %get-tuple-element.29), channel_id=1, source_target_pairs={{0,1},{1,0},{2,3},{3,2},{4,5},{5,4},{6,7},{7,6},{8,9},{9,8},{10,11... | collective-permute-start | bytes 98312 | tf_op jit(solution)/shard_map/ppermute | solution.py:332
  4.8 4.2 %collective-permute-start.1 = (f32[64,128]{1,0:T(8,128)S(1)}, f32[64,128]{1,0:T(8,128)S(1)}, u32[]{:S(2)}, u32[]{:S(2)}) collective-permute-start(f32[64,128]{1,0:T(8,128)S(1)} %add.24.refs_0_), channel_id=1, source_target_pairs={{0,3},{1,2},{2,1},{3,0},{4,7},{5,6},{6,5},{7,4},{8,11},{9,10},{10,... | collective-permute-start | bytes 98312 | tf_op jit(solution)/shard_map/ppermute | solution.py:332
  9.5 8.1 %collective-permute-start.2 = (f32[264,128]{1,0:T(8,128)S(1)}, f32[264,128]{1,0:T(8,128)S(1)}, u32[]{:S(2)}, u32[]{:S(2)}) collective-permute-start(f32[264,128]{1,0:T(8,128)S(1)} %get-tuple-element.36), channel_id=1, source_target_pairs={{0,4},{1,5},{2,6},{3,7},{4,0},{5,1},{6,2},{7,3},{8,12},{9,13},{10,... | collective-permute-start | bytes 405512 | tf_op jit(solution)/shard_map/ppermute | solution.py:332
  11.6 6.5 %collective-permute-start.3 = (f32[264,128]{1,0:T(8,128)S(1)}, f32[264,128]{1,0:T(8,128)S(1)}, u32[]{:S(2)}, u32[]{:S(2)}) collective-permute-start(f32[264,128]{1,0:T(8,128)S(1)} %get-tuple-element.37), channel_id=1, source_target_pairs={{0,8},{1,9},{2,10},{3,11},{4,12},{5,13},{6,14},{7,15},{8,0},{9,1},... | collective-permute-start | bytes 405512 | tf_op jit(solution)/shard_map/ppermute | solution.py:332
  13.2 10.6 %collective-permute-start.5 = (f32[264,128]{1,0:T(8,128)S(1)}, f32[264,128]{1,0:T(8,128)S(1)}, u32[]{:S(2)}, u32[]{:S(2)}) collective-permute-start(f32[264,128]{1,0:T(8,128)S(1)} %get-tuple-element.41), channel_id=1, source_target_pairs={{0,8},{1,9},{2,10},{3,11},{4,12},{5,13},{6,14},{7,15},{8,0},{9,1},... | collective-permute-start | bytes 405512 | tf_op jit(solution)/shard_map/ppermute | solution.py:332
  13.6 12.4 %collective-permute-start.6 = (f32[264,128]{1,0:T(8,128)S(1)}, f32[264,128]{1,0:T(8,128)S(1)}, u32[]{:S(2)}, u32[]{:S(2)}) collective-permute-start(f32[264,128]{1,0:T(8,128)S(1)} %get-tuple-element.42), channel_id=1, source_target_pairs={{0,28},{1,29},{2,30},{3,31},{4,24},{5,25},{6,26},{7,27},{8,20},{9,... | collective-permute-start | bytes 405512 | tf_op jit(solution)/shard_map/ppermute | solution.py:332
  18.1 11.0 %collective-permute-start.4 = (f32[264,128]{1,0:T(8,128)S(1)}, f32[264,128]{1,0:T(8,128)S(1)}, u32[]{:S(2)}, u32[]{:S(2)}) collective-permute-start(f32[264,128]{1,0:T(8,128)S(1)} %add.26), channel_id=1, source_target_pairs={{0,16},{1,17},{2,18},{3,19},{4,20},{5,21},{6,22},{7,23},{8,24},{9,... | collective-permute-start | bytes 405512 | tf_op jit(solution)/shard_map/ppermute | solution.py:332
  20.8 8.3 %collective-permute-start.7 = (f32[264,128]{1,0:T(8,128)S(1)}, f32[264,128]{1,0:T(8,128)S(1)}, u32[]{:S(2)}, u32[]{:S(2)}) collective-permute-start(f32[264,128]{1,0:T(8,128)S(1)} %get-tuple-element.43), channel_id=1, source_target_pairs={{0,12},{1,13},{2,14},{3,15},{4,8},{5,9},{6,10},{7,11},{8,4},{9,5},... | collective-permute-start | bytes 405512 | tf_op jit(solution)/shard_map/ppermute | solution.py:332
  22.3 7.9 %collective-permute-start.8 = (f32[264,128]{1,0:T(8,128)S(1)}, f32[264,128]{1,0:T(8,128)S(1)}, u32[]{:S(2)}, u32[]{:S(2)}) collective-permute-start(f32[264,128]{1,0:T(8,128)S(1)} %get-tuple-element.44), channel_id=1, source_target_pairs={{0,4},{1,5},{2,6},{3,7},{4,0},{5,1},{6,2},{7,3},{8,12},{9,13},{10,... | collective-permute-start | bytes 405512 | tf_op jit(solution)/shard_map/ppermute | solution.py:332
  30.6 1.2 %collective-permute-start.9 = (f32[32,128]{1,0:T(8,128)S(1)}, f32[32,128]{1,0:T(8,128)S(1)}, u32[]{:S(2)}, u32[]{:S(2)}) collective-permute-start(f32[32,128]{1,0:T(8,128)S(1)} %get-tuple-element.45), channel_id=1, source_target_pairs={{0,1},{1,0},{2,3},{3,2},{4,5},{5,4},{6,7},{7,6},{8,9},{9,8},{10,11... | collective-permute-start | bytes 49160 | tf_op jit(solution)/shard_map/ppermute | solution.py:332
  31.8 4.1 %collective-permute-start.12 = (f32[32,128]{1,0:T(8,128)S(1)}, f32[32,128]{1,0:T(8,128)S(1)}, u32[]{:S(2)}, u32[]{:S(2)}) collective-permute-start(f32[32,128]{1,0:T(8,128)S(1)} %add.27), channel_id=1, source_target_pairs={{0,7},{1,6},{2,5},{3,4},{4,3},{5,2},{6,1},{7,0},{8,15},{9,14},{10,... | collective-permute-start | bytes 49160 | tf_op jit(solution)/shard_map/ppermute | solution.py:332
  34.0 3.2 %collective-permute-start.11 = (f32[32,128]{1,0:T(8,128)S(1)}, f32[32,128]{1,0:T(8,128)S(1)}, u32[]{:S(2)}, u32[]{:S(2)}) collective-permute-start(f32[32,128]{1,0:T(8,128)S(1)} %add.27), channel_id=1, source_target_pairs={{0,5},{1,4},{2,7},{3,6},{4,1},{5,0},{6,3},{7,2},{8,13},{9,12},{10,... | collective-permute-start | bytes 49160 | tf_op jit(solution)/shard_map/ppermute | solution.py:332
  34.5 3.2 %collective-permute-start.10 = (f32[32,128]{1,0:T(8,128)S(1)}, f32[32,128]{1,0:T(8,128)S(1)}, u32[]{:S(2)}, u32[]{:S(2)}) collective-permute-start(f32[32,128]{1,0:T(8,128)S(1)} %add.27), channel_id=1, source_target_pairs={{0,3},{1,2},{2,1},{3,0},{4,7},{5,6},{6,5},{7,4},{8,11},{9,10},{10,... | collective-permute-start | bytes 49160 | tf_op jit(solution)/shard_map/ppermute | solution.py:332
  37.7 3.2 %collective-permute-start.13 = (f32[32,128]{1,0:T(8,128)S(1)}, f32[32,128]{1,0:T(8,128)S(1)}, u32[]{:S(2)}, u32[]{:S(2)}) collective-permute-start(f32[32,128]{1,0:T(8,128)S(1)} %add_add_fusion), channel_id=1, source_target_pairs={{0,9},{1,8},{2,11},{3,10},{4,13},{5,12},{6,15},{7,14},{8,1},{9,0},... | collective-permute-start | bytes 49160 | tf_op jit(solution)/shard_map/ppermute | solution.py:332
  40.9 4.1 %collective-permute-start.14 = (f32[32,128]{1,0:T(8,128)S(1)}, f32[32,128]{1,0:T(8,128)S(1)}, u32[]{:S(2)}, u32[]{:S(2)}) collective-permute-start(f32[32,128]{1,0:T(8,128)S(1)} %add.31.gram_ref.refs_0_), channel_id=1, source_target_pairs={{0,17},{1,16},{2,19},{3,18},{4,21},{5,20},{6,23},{7,22},{8,25},{9,... | collective-permute-start | bytes 49160 | tf_op jit(solution)/shard_map/ppermute | solution.py:332
